TPU v7x, 32 devices: a whole 2x2x4 slice. The times are simulated.
32 devices in a mesh: pole: 2 (over x), prow: 2 (over core), pcol: 8 (over z, y).
Axes of the slice: x: 2, y: 2, z: 4, core: 2. Of those that a mesh axis runs over, the one named last changes fastest.
Arguments:
- inverse_blocks: bfloat16 [16, 512, 4096], P('pole', 'prow', 'pcol'), parts along dimension 0, may hold values from -6 to 6
- lower: bfloat16 [32, 3, 512, 512], P('pole', None, ('prow', 'pcol')), parts along dimension 0, may hold values from -0.15625 to 0.15625
- diag_inverse: float32 [32, 512, 512], P('pole', ('prow', 'pcol')), parts along dimension 0, may hold values from -6 to 6
- structure: int32 [32, 3], P('pole'), parts along dimension 0, may hold values from 0 to 7, as said below
Outputs:
- diag_blocks: float32 [32, 512, 512], P('pole', ('prow', 'pcol')), parts along dimension 0
There are 2 independent parts, one for each index of `pole`. A program takes and returns all parts, laid end to end along the dimension named above; each array names one. Nothing has to cross between parts.
Inputs may be any that keep to these rules, and one draw needn't show every extreme that they name: `structure`: each row names 3 different trailing supernodes; one trailing supernode is named by exactly 7 rows and none by more.
All inputs are finite; a program needn't handle non-finite values.
Results may differ from a plain program's by a relative error of at most 0.0021.
Values may be sent and summed in bfloat16 or wider, within the bound.
A program may use at most 128 MiB of HBM per device.

v0:
```python
import jax
import jax.numpy as jnp
from jax import lax
from jax.sharding import PartitionSpec as P

B = 512


def per_device(inverse_blocks, lower, diag_inverse, structure):
    columns = lax.axis_size("pcol")
    own_column = lax.axis_index("pcol")
    node_count = structure.shape[0]
    slots_each = structure.shape[1]
    cap_slots = max(
        2, max(node_count // 4, (slots_each * node_count + columns - 2) // (columns - 1))
    )
    matches = structure[None, :, :] == jnp.arange(columns, dtype=jnp.int32)[:, None, None]
    present = jnp.any(matches, axis=2)
    position = jnp.cumsum(present.astype(jnp.int32), axis=1) - 1
    slot_match = present[:, :, None] & (
        position[:, :, None] == jnp.arange(cap_slots, dtype=jnp.int32)[None, None, :]
    )
    task_table = jnp.sum(
        slot_match.astype(jnp.int32) * jnp.arange(node_count, dtype=jnp.int32)[None, :, None],
        axis=1,
    )
    valid = jnp.any(slot_match, axis=1)
    my_tasks = lax.dynamic_index_in_dim(task_table, own_column, 0, False)
    my_valid = lax.dynamic_index_in_dim(valid, own_column, 0, False)
    flipped = jnp.swapaxes(lower, 0, 1)
    gathered = lax.all_gather(flipped, "pcol", axis=2, tiled=True)
    halves = gathered[:, my_tasks] * my_valid[None, :, None, None].astype(jnp.bfloat16)
    task_lists = structure[my_tasks]
    pick = (task_lists == own_column).astype(jnp.bfloat16)
    own_half = jnp.einsum("cs,scrb->crb", pick, halves, preferred_element_type=jnp.float32).astype(
        jnp.bfloat16
    )
    own_full = lax.all_gather(own_half, "prow", axis=1, tiled=True)
    contribs = []
    for index_slot in range(cap_slots):
        chosen = inverse_blocks[task_lists[index_slot]]
        products = jnp.einsum(
            "sab,bc->sac", chosen, own_full[index_slot], preferred_element_type=jnp.float32
        ).astype(jnp.bfloat16)
        contribs.append(
            jnp.einsum(
                "sba,sbc->ac", halves[:, index_slot], products, preferred_element_type=jnp.float32
            )
        )
    totals = jnp.zeros((node_count, B, B), jnp.float32)
    for index_slot in range(cap_slots):
        supernode = my_tasks[index_slot]
        current = lax.dynamic_index_in_dim(totals, supernode, 0, False)
        totals = lax.dynamic_update_index_in_dim(
            totals, current + contribs[index_slot], supernode, 0
        )
    coupling = lax.psum_scatter(totals, ("prow", "pcol"), scatter_dimension=1, tiled=True)
    return diag_inverse - coupling


def solution(mesh):
    placed = (
        P("pole", "prow", "pcol"),
        P("pole", None, ("prow", "pcol"), None),
        P("pole", ("prow", "pcol"), None),
        P("pole", None),
    )
    return jax.shard_map(
        per_device,
        mesh=mesh,
        in_specs=placed,
        out_specs=P("pole", ("prow", "pcol"), None),
        check_vma=False,
    )
```

profile of v0, /device:TPU:0, one launch (start us, length us, event | category | flops | bytes accessed | tf_op | source)
XLA Modules:
  0.0 479.3 jit_solution(14561414702946972345)
XLA Ops:
  6.5 2.9 copy.25
  9.5 0.0 all-gather.3.cloned.1.call-update
  9.5 0.0 all-gather.5.cloned.1.call-start
  9.5 0.8 copy.16
  10.3 0.7 fusion.23
  11.0 0.2 reduce_window_sum.11
  11.2 0.2 fusion.20
  11.4 0.2 fusion.24
  11.6 0.2 select_reduce_fusion
  11.8 0.2 fusion.33
  12.0 0.6 gather_fusion.1
  12.6 176.2 %all-gather.3.cloned.1.call-done = bf16[3,16,256,512]{3,2,1,0:T(8,128)(2,1)} async-done(((bf16[3,16,32,512]{3,2,1,0:T(8,128)(2,1)}), bf16[3,16,256,512]{3,2,1,0:T(8,128)(2,1)}) %all-gather.3.cloned.1.call-update) | async-done | bytes 12582928 | tf_op jit(solution)/shard_map/all_gather | solution.py:31
  188.8 7.9 %gather_fusion = bf16[7,3,256,512]{3,2,1,0:T(8,128)(2,1)} fusion(bf16[3,16,256,512]{3,2,1,0:T(8,128)(2,1)} %all-gather.3.cloned.1.call-done, s32[1024]{0:T(1024)S(1)} %pad_clamp_fusion.7), kind=kCustom, calls=%fused_computation | custom fusion | bytes 11010076 | tf_op jit(solution)/shard_map/gather | solution.py:32
  196.7 8.3 %copy.15 = bf16[7,3,256,512]{2,3,1,0:T(8,128)(2,1)} copy(bf16[7,3,256,512]{3,2,1,0:T(8,128)(2,1)} %gather_fusion) | data formatting | bytes 11010048 | tf_op jit(solution)/shard_map/gather | solution.py:32
  205.0 5.4 %multiply_bitcast_fusion = bf16[3,7,256,512]{2,3,0,1:T(8,128)(2,1)} fusion(bf16[7,3,256,512]{2,3,1,0:T(8,128)(2,1)} %copy.15, bf16[7]{0:T(256)(128)(2,1)S(1)} %fusion.24), kind=kLoop, calls=%fused_computation.9 | loop fusion | flops 2752512 | bytes 11010062 | tf_op jit(solution)/shard_map/mul | solution.py:32
  210.4 12.5 %copy.18 = bf16[3,7,256,512]{3,0,2,1:T(4,128)(2,1)} copy(bf16[3,7,256,512]{2,3,0,1:T(8,128)(2,1)} %multiply_bitcast_fusion) | data formatting | bytes 11010048 | tf_op jit(solution)/shard_map/mul | solution.py:32
  222.8 6.2 %fusion.21 = bf16[7,1,256,512]{3,1,2,0:T(2,128)(2,1)S(1)} fusion(bf16[3,7,256,512]{3,0,2,1:T(4,128)(2,1)} %copy.18, pred[7,3,1,1]{1,0,2,3:T(8,128)(4,1)S(1)} %compare_bitcast_fusion), kind=kOutput, calls=%fused_computation.63 | convolution fusion | flops 5505024 | bytes 7340053 | tf_op jit(solution)/shard_map/cs,scrb->crb/dot_general | solution.py:35
  229.0 1.8 copy.24
  230.8 0.0 all-gather.5.cloned.1.call-update
  230.8 0.0 reduce-scatter.2.cloned.1.call-start
  230.9 0.6 fusion.34
  239.9 1.5 gather_fusion.2
  241.4 1.5 gather_fusion.3
  243.0 1.5 gather_fusion.4
  244.5 1.5 gather_fusion.5
  246.0 1.5 gather_fusion.6
  247.5 1.5 gather_fusion.7
  249.0 0.6 gather_fusion.8
  253.9 0.0 copy-start.5
  253.9 0.0 all-gather.5.cloned.1.call-done
  253.9 8.0 %broadcast_in_dim.41 = f32[16,512,512]{2,1,0:T(8,128)} broadcast(f32[]{:T(128)} %constant.56.clone.1), dimensions={} | broadcast | bytes 16777220 | tf_op jit(solution)/shard_map/broadcast_in_dim | solution.py:50
  261.9 3.2 fusion
  265.2 1.4 constant_dynamic-slice_fusion.5
  266.5 3.5 fusion.3
  270.0 1.3 constant_dynamic-slice_fusion.4
  271.3 3.2 fusion.6
  274.6 1.4 constant_dynamic-slice_fusion.3
  275.9 3.5 fusion.9
  279.4 1.3 constant_dynamic-slice_fusion.2
  280.7 3.2 fusion.12
  283.9 1.3 constant_dynamic-slice_fusion.1
  285.2 3.5 fusion.15
  288.7 1.3 constant_dynamic-slice_fusion
  290.0 3.3 fusion.18
  293.3 0.0 reduce-scatter.2.cloned.1.call-update
  293.3 0.0 copy-start.1
  293.3 177.0 %reduce-scatter.2.cloned.1.call-done = f32[16,32,512]{2,1,0:T(8,128)} async-done(((f32[16,512,512]{2,1,0:T(8,128)}), f32[16,32,512]{2,1,0:T(8,128)}) %reduce-scatter.2.cloned.1.call-update) | async-done | bytes 1048592 | tf_op jit(solution)/shard_map/reduce_scatter | solution.py:57
  470.4 2.4 sub.8
  (21 shorter events, 0.1 us)
Async XLA Ops:
  6.5 233.4 %copy-start = (bf16[8,256,512]{2,1,0:T(8,128)(2,1)S(1)}, bf16[8,256,512]{2,1,0:T(8,128)(2,1)}, u32[]{:S(2)}) copy-start(bf16[8,256,512]{2,1,0:T(8,128)(2,1)} %param.4) | copy-start | bytes 6291460
  6.5 182.2 %all-gather.3.cloned.1.call-start = ((), (), s32[]{:S(2)}) async-start(), calls=%async_computation.1 | async-start | bytes 14155776 | tf_op jit(solution)/shard_map/all_gather | solution.py:31
  9.5 244.4 %all-gather.5.cloned.1.call-start = ((), (), s32[]{:S(2)}) async-start(), calls=%async_computation.2 | async-start | bytes 5505024 | tf_op jit(solution)/shard_map/all_gather | solution.py:38
  230.8 239.6 %reduce-scatter.2.cloned.1.call-start = ((), (), s32[]{:S(2)}) async-start(), calls=%async_computation.3 | async-start | bytes 17825792 | tf_op jit(solution)/shard_map/reduce_scatter | solution.py:57
  253.9 8.0 %copy-start.5 = (bf16[3,256,512]{2,1,0:T(8,128)(2,1)S(1)}, bf16[3,256,512]{2,1,0:T(8,128)(2,1)}, u32[]{:S(2)}) copy-start(bf16[3,256,512]{2,1,0:T(8,128)(2,1)} %gather_fusion.2) | copy-start | bytes 2359300
  265.2 6.2 %copy-start.4 = (bf16[3,256,512]{2,1,0:T(8,128)(2,1)S(1)}, bf16[3,256,512]{2,1,0:T(8,128)(2,1)}, u32[]{:S(2)}) copy-start(bf16[3,256,512]{2,1,0:T(8,128)(2,1)} %gather_fusion.4) | copy-start | bytes 2359300
  274.6 6.1 %copy-start.3 = (bf16[3,256,512]{2,1,0:T(8,128)(2,1)S(1)}, bf16[3,256,512]{2,1,0:T(8,128)(2,1)}, u32[]{:S(2)}) copy-start(bf16[3,256,512]{2,1,0:T(8,128)(2,1)} %gather_fusion.6) | copy-start | bytes 2359300
  293.3 177.1 %copy-start.2 = (f32[16,32,512]{2,1,0:T(8,128)S(1)}, f32[16,32,512]{2,1,0:T(8,128)}, u32[]{:S(2)}) copy-start(f32[16,32,512]{2,1,0:T(8,128)} %param.6) | copy-start | bytes 3145732
  293.3 179.5 %copy-start.1 = (bf16[8,256,512]{2,1,0:T(8,128)(2,1)S(1)}, bf16[8,256,512]{2,1,0:T(8,128)(2,1)}, u32[]{:S(2)}) copy-start(bf16[8,256,512]{2,1,0:T(8,128)(2,1)} %param.4) | copy-start | bytes 6291460
Sparse Core Ops, SparseCore 0:
  9.6 179.1 all-gather.2
  230.9 11.0 all-gather.4
  293.4 176.8 reduce-scatter.1
where the time goes:
time: 481 us; the launch traced here: 479 us
  waiting for transfers between devices  353 us (73%)
  local copies, waits for them, and re-layouts  61.1 us (13%)
  matrix products  29.6 us (6%)
  between operations  25.9 us (5%)
  other arithmetic  9.32 us (2%)
    reduce_scatter x1, waiting for transfers between devices, per_device(): lax.psum_scatter(totals, ('prow', 'pcol'), scatter_dimension=1, tiled=True)  177 us
    all_gather x1, waiting for transfers between devices, per_device(): gathered = lax.all_gather(flipped, 'pcol', axis=2, tiled=True)  176 us
    dot_general x7, matrix products, per_device(): jnp.einsum('sba,sbc->ac', halves[:, index_slot], products, preferred_elem...  23.4 us
    gather x2, local copies, waits for them, and re-layouts, per_device(): gathered[:, my_tasks] * my_valid[None, :, None, None].astype(jnp.bfloat16)  16.2 us
    mul x1, local copies, waits for them, and re-layouts, per_device(): gathered[:, my_tasks] * my_valid[None, :, None, None].astype(jnp.bfloat16)  12.5 us
    gather x7, local copies, waits for them, and re-layouts, per_device(): chosen = inverse_blocks[task_lists[index_slot]]  9.69 us
  transfers between devices with their start and end apart: 3, of which 2 were waited for; matrix products, arithmetic and copies ran while one was open for 3% of the time, Pallas kernels for 0%

commit v1 on v0

--- a/solution.py
+++ b/solution.py
@@ -1,6 +1,10 @@
+import functools
+
 import jax
 import jax.numpy as jnp
 from jax import lax
+from jax.experimental import pallas as pl
+from jax.experimental.pallas import tpu as pltpu
 from jax.sharding import PartitionSpec as P
 
 B = 512
@@ -58,6 +62,236 @@
     return diag_inverse - coupling
 
 
+MESH = pl.DeviceIdType.MESH
+
+
+def fused_kernel(
+    columns, cap, nodes, slots,
+    tasks, own_slot, structure, places,
+    inverse_ref, lower_ref, diag_ref,
+    out_ref,
+    picked, halves, full, partial, from_core, outgoing, incoming,
+    pick_send, pick_recv, half_send, half_recv, core_send, core_recv, out_send, out_recv,
+):
+    pole = lax.axis_index("pole")
+    core = lax.axis_index("prow")
+    me = lax.axis_index("pcol")
+    other = 1 - core
+    peers = columns - 1
+
+    barrier = pltpu.get_barrier_semaphore()
+
+    def greet(step, carry):
+        peer = lax.rem(me + 1 + step, columns)
+        pl.semaphore_signal(barrier, inc=1, device_id=(pole, core, peer), device_id_type=MESH)
+        return carry
+
+    lax.fori_loop(0, peers, greet, 0)
+    pl.semaphore_signal(barrier, inc=1, device_id=(pole, other, me), device_id_type=MESH)
+    pl.semaphore_wait(barrier, columns)
+
+    def pick_copy(index, step):
+        peer = lax.rem(me + 1 + step, columns)
+        return pltpu.make_async_remote_copy(
+            src_ref=picked.at[index, step],
+            dst_ref=halves.at[index, me],
+            send_sem=pick_send.at[index, step],
+            recv_sem=pick_recv.at[index, step],
+            device_id=(pole, core, peer),
+            device_id_type=MESH,
+        )
+
+    def half_copy(index):
+        return pltpu.make_async_remote_copy(
+            src_ref=full.at[index, core],
+            dst_ref=full.at[index, core],
+            send_sem=half_send.at[index],
+            recv_sem=half_recv.at[index],
+            device_id=(pole, other, me),
+            device_id_type=MESH,
+        )
+
+    def core_copy(index):
+        return pltpu.make_async_remote_copy(
+            src_ref=partial.at[index, other],
+            dst_ref=from_core.at[index],
+            send_sem=core_send.at[index],
+            recv_sem=core_recv.at[index],
+            device_id=(pole, other, me),
+            device_id_type=MESH,
+        )
+
+    def out_copy(index, step):
+        peer = lax.rem(me + 1 + step, columns)
+        return pltpu.make_async_remote_copy(
+            src_ref=outgoing.at[index, peer],
+            dst_ref=incoming.at[me, index],
+            send_sem=out_send.at[index, step],
+            recv_sem=out_recv.at[index, step],
+            device_id=(pole, core, peer),
+            device_id_type=MESH,
+        )
+
+    def send_task(index, carry):
+        def to_peer(step, inner):
+            peer = lax.rem(me + 1 + step, columns)
+            picked[index, step] = lower_ref[tasks[peer * cap + index]]
+            pick_copy(index, step).start()
+            return inner
+
+        lax.fori_loop(0, peers, to_peer, 0)
+        halves[index, me] = lower_ref[tasks[me * cap + index]]
+        return carry
+
+    lax.fori_loop(0, cap, send_task, 0)
+
+    def arrive(index):
+        def one(step, inner):
+            pick_copy(index, step).wait_recv()
+            return inner
+
+        lax.fori_loop(0, peers, one, 0)
+        chosen_slot = own_slot[me * cap + index]
+        mine = halves[index, :, 0]
+        for slot in range(1, slots):
+            mine = jnp.where(chosen_slot == slot, halves[index, :, slot], mine)
+        full[index, core] = mine.reshape(full.shape[2:])
+        half_copy(index).start()
+
+    def multiply(index):
+        half_copy(index).wait_recv()
+        node = tasks[me * cap + index]
+        factor = full[index].reshape(B, B)
+        total = jnp.zeros((B, B), jnp.float32)
+        for slot in range(slots):
+            chosen = inverse_ref[structure[node * slots + slot]]
+            products = jnp.dot(chosen, factor, preferred_element_type=jnp.float32).astype(
+                jnp.bfloat16
+            )
+            rows = halves[index, :, slot].reshape(B // 2, B)
+            total = total + lax.dot_general(
+                rows, products, (((0,), (0,)), ((), ())), preferred_element_type=jnp.float32
+            )
+        partial[index] = total.reshape(partial.shape[1:])
+        core_copy(index).start()
+
+    def hand_out(index):
+        core_copy(index).wait_recv()
+        summed = (partial[index, core] + from_core[index]).astype(jnp.bfloat16)
+        outgoing[index] = summed.reshape(outgoing.shape[1:])
+        incoming[me, index] = outgoing[index, me]
+
+        def one(step, inner):
+            out_copy(index, step).start()
+            return inner
+
+        lax.fori_loop(0, peers, one, 0)
+
+    def step_all(step, carry):
+        @pl.when(step < cap)
+        def _():
+            arrive(step)
+
+        @pl.when((step >= 1) & (step < cap + 1))
+        def _():
+            multiply(step - 1)
+
+        @pl.when(step >= 2)
+        def _():
+            hand_out(step - 2)
+
+        return carry
+
+    lax.fori_loop(0, cap + 2, step_all, 0)
+
+    def landed(index, carry):
+        def one(step, inner):
+            out_copy(index, step).wait_recv()
+            return inner
+
+        lax.fori_loop(0, peers, one, 0)
+        return carry
+
+    lax.fori_loop(0, cap, landed, 0)
+
+    def finish(node, carry):
+        value = jnp.zeros(out_ref.shape[1:], jnp.float32)
+        for slot in range(slots):
+            place = node * slots + slot
+            value = value + incoming[structure[place], places[place]].astype(jnp.float32)
+        out_ref[node] = diag_ref[node] - value
+        return carry
+
+    lax.fori_loop(0, nodes, finish, 0)
+
+    def sent(index, carry):
+        def one(step, inner):
+            pick_copy(index, step).wait_send()
+            out_copy(index, step).wait_send()
+            return inner
+
+        lax.fori_loop(0, peers, one, 0)
+        half_copy(index).wait_send()
+        core_copy(index).wait_send()
+        return carry
+
+    lax.fori_loop(0, cap, sent, 0)
+
+
+def per_device_fused(inverse_blocks, lower, diag_inverse, structure):
+    columns = lax.axis_size("pcol")
+    nodes, slots = structure.shape
+    chunk = lower.shape[2]
+    cap = max(2, max(nodes // 4, (slots * nodes + columns - 2) // (columns - 1)))
+    node_ids = jnp.arange(nodes, dtype=jnp.int32)
+    matches = structure[None] == jnp.arange(columns, dtype=jnp.int32)[:, None, None]
+    present = jnp.any(matches, axis=2)
+    earlier = node_ids[None, :] < node_ids[:, None]
+    position = jnp.sum((present[:, None, :] & earlier[None]).astype(jnp.int32), axis=2)
+    hit = present[:, None, :] & (
+        position[:, None, :] == jnp.arange(cap, dtype=jnp.int32)[None, :, None]
+    )
+    tasks = jnp.sum(jnp.where(hit, node_ids[None, None, :], 0), axis=2)
+    slot_of = jnp.sum(
+        jnp.where(matches, jnp.arange(slots, dtype=jnp.int32)[None, None, :], 0), axis=2
+    )
+    own_slot = jnp.sum(jnp.where(hit, slot_of[:, None, :], 0), axis=2)
+    places = jnp.sum(jnp.where(matches, position[:, :, None], 0), axis=0)
+    smem = pl.BlockSpec(memory_space=pltpu.SMEM)
+    vmem = pl.BlockSpec(memory_space=pltpu.VMEM)
+    peers = columns - 1
+    dma = pltpu.SemaphoreType.DMA
+    return pl.pallas_call(
+        functools.partial(fused_kernel, columns, cap, nodes, slots),
+        out_shape=jax.ShapeDtypeStruct(diag_inverse.shape, jnp.float32),
+        in_specs=[smem] * 4 + [vmem] * 3,
+        out_specs=vmem,
+        scratch_shapes=[
+            pltpu.VMEM((cap, peers, slots, chunk, B), jnp.bfloat16),
+            pltpu.VMEM((cap, columns, slots, chunk, B), jnp.bfloat16),
+            pltpu.VMEM((cap, 2, B // 2, B), jnp.bfloat16),
+            pltpu.VMEM((cap, 2, B // 2, B), jnp.float32),
+            pltpu.VMEM((cap, B // 2, B), jnp.float32),
+            pltpu.VMEM((cap, columns, chunk, B), jnp.bfloat16),
+            pltpu.VMEM((columns, cap, chunk, B), jnp.bfloat16),
+            dma((cap, peers)),
+            dma((cap, peers)),
+            dma((cap,)),
+            dma((cap,)),
+            dma((cap,)),
+            dma((cap,)),
+            dma((cap, peers)),
+            dma((cap, peers)),
+        ],
+        compiler_params=pltpu.CompilerParams(
+            collective_id=0, has_side_effects=True, vmem_limit_bytes=48 * 1024 * 1024
+        ),
+    )(
+        tasks.reshape(-1), own_slot.reshape(-1), structure.reshape(-1), places.reshape(-1),
+        inverse_blocks, lower, diag_inverse,
+    )
+
+
 def solution(mesh):
     placed = (
         P("pole", "prow", "pcol"),
@@ -65,8 +299,12 @@
         P("pole", ("prow", "pcol"), None),
         P("pole", None),
     )
+    body = per_device
+    whole_tiles = B % (16 * mesh.shape["prow"] * mesh.shape["pcol"]) == 0
+    if mesh.shape["prow"] == 2 and mesh.shape["pcol"] == 8 and whole_tiles:
+        body = per_device_fused
     return jax.shard_map(
-        per_device,
+        body,
         mesh=mesh,
         in_specs=placed,
         out_specs=P("pole", ("prow", "pcol"), None),

time: 481 us -> 175 us (0.36)
  waiting for transfers between devices: 353 us -> 0 us
  Pallas kernels: 0 us -> 167 us
  local copies, waits for them, and re-layouts: 61.1 us -> 6.55 us
  matrix products: 29.6 us -> 0 us
  between operations: 25.9 us -> 0.04 us
  other arithmetic: 9.32 us -> 1.93 us
    reduce_scatter x1 -> x0, waiting for transfers between devices: 177 us -> none  [per_device(): lax.psum_scatter(totals, ('prow', 'pcol'), scatter_dimension=1, tiled=True)]
    all_gather x2 -> x0, waiting for transfers between devices: 176 us -> none  [the longest x1 176 us: per_device(): gathered = lax.all_gather(flipped, 'pcol', axis=2, tiled=True)]
    pallas_call x0 -> x1, Pallas kernels: none -> 167 us  [per_device_fused(): pl.pallas_call(functools.partial(fused_kernel, columns, cap, nodes, slots...]
    dot_general x8 -> x0, matrix products: 29.6 us -> none  [the longest x7 23.4 us: per_device(): jnp.einsum('sba,sbc->ac', halves[:, index_slot], products, preferred_elem...]
    gather x10 -> x0, local copies, waits for them, and re-layouts: 26.5 us -> none  [the longest x2 16.2 us: per_device(): gathered[:, my_tasks] * my_valid[None, :, None, None].astype(jnp.bfloat16)]
    mul x1 -> x0, local copies, waits for them, and re-layouts: 12.5 us -> none  [per_device(): gathered[:, my_tasks] * my_valid[None, :, None, None].astype(jnp.bfloat16)]
    dynamic_slice x7 -> x0, local copies, waits for them, and re-layouts: 8.09 us -> none  [the longest x6 7.9 us: per_device(): current = lax.dynamic_index_in_dim(totals, supernode, 0, False)]
    broadcast_in_dim x1 -> x0, local copies, waits for them, and re-layouts: 8 us -> none  [per_device(): totals = jnp.zeros((node_count, B, B), jnp.float32)]
  transfers between devices with their start and end apart: 3 -> 0, of which waited for: 2 -> 0; matrix products, arithmetic and copies ran while one was open for 3% -> 0% of each run, Pallas kernels for 0% -> 0%
where the time goes in v1:
time: 175 us
  Pallas kernels  167 us (95%)
  local copies, waits for them, and re-layouts  6.55 us (4%)
  other arithmetic  1.93 us (1%)
    pallas_call x1, Pallas kernels, per_device_fused(): pl.pallas_call(functools.partial(fused_kernel, columns, cap, nodes, slots...  167 us
    unnamed x8, local copies, waits for them, and re-layouts  5.95 us

profile of v1, /device:TPU:0, one launch (start us, length us, event | category | flops | bytes accessed | tf_op | source)
XLA Modules:
  0.0 175.0 jit_solution(513778701129367426)
XLA Ops:
  0.0 0.7 fusion.1
  0.7 0.2 convert_reduce_fusion
  0.9 0.7 select_reduce_fusion.2
  1.6 0.3 select_reduce_fusion
  1.9 0.1 copy.10
  2.0 0.1 reshape.30.own_slot
  2.1 0.1 copy.9
  2.2 0.1 reshape.29.tasks
  2.3 0.1 copy.12
  2.3 0.1 reshape.32.places
  2.4 0.8 copy.11
  3.2 0.1 reshape.31.structure
  3.3 0.0 copy-start
  3.3 1.6 copy-done
  4.9 0.0 copy-start.1
  4.9 1.4 copy-done.1
  6.3 0.0 copy-start.2
  6.3 1.2 copy-done.2
  7.5 166.5 %shard_map.46 = f32[16,32,512]{2,1,0:T(8,128)S(1)} custom-call(s32[56]{0:T(128)S(1)} %reshape.29.tasks, s32[56]{0:T(128)S(1)} %reshape.30.own_slot, s32[48]{0:T(128)S(1)} %reshape.31.structure, s32[48]{0:T(128)S(1)} %reshape.32.places, bf16[8,256,512]{2,1,0:T(8,128)(2,1)S(1)} %copy-done, bf16[16,3,32,512]{3,2,1,0:T(8,128)(2,1)S(1)} %copy-done.1, ...), custom_call_target="tpu_custom_call" | custom-call | tf_op jit(solution)/shard_map/pallas_call | solution.py:264
  174.1 1.0 copy.14
  (1 shorter events, 0.0 us)
Async XLA Ops:
  3.3 1.6 copy-start
  4.9 1.4 copy-start.1
  6.3 1.2 copy-start.2

commit v2 on v1

--- a/solution.py
+++ b/solution.py
@@ -68,16 +68,24 @@
 def fused_kernel(
     columns, cap, nodes, slots,
     tasks, own_slot, structure, places,
-    inverse_ref, lower_ref, diag_ref,
+    inverse_hbm, lower_ref, diag_hbm,
     out_ref,
-    picked, halves, full, partial, from_core, outgoing, incoming,
-    pick_send, pick_recv, half_send, half_recv, core_send, core_recv, out_send, out_recv,
+    inverse_ref, diag_ref, mirrored, picked, halves, full, partial, from_core, outgoing, incoming,
+    load_sem, mirror_send, mirror_recv, pick_send, pick_recv, half_send, half_recv, core_send, core_recv, out_send, out_recv,
 ):
     pole = lax.axis_index("pole")
     core = lax.axis_index("prow")
     me = lax.axis_index("pcol")
     other = 1 - core
     peers = columns - 1
+    mates = columns // 2 - 1
+    base = (me // (mates + 1)) * (mates + 1)
+    mirror = columns - 2 - me + 2 * (me % 2)
+    parts = mirror_send.shape[0]
+    span = nodes // parts
+
+    load_inverse = pltpu.make_async_copy(inverse_hbm, inverse_ref, load_sem.at[0])
+    load_diag = pltpu.make_async_copy(diag_hbm, diag_ref, load_sem.at[1])
 
     barrier = pltpu.get_barrier_semaphore()
 
@@ -90,14 +98,27 @@
     pl.semaphore_signal(barrier, inc=1, device_id=(pole, other, me), device_id_type=MESH)
     pl.semaphore_wait(barrier, columns)
 
-    def pick_copy(index, step):
-        peer = lax.rem(me + 1 + step, columns)
-        return pltpu.make_async_remote_copy(
-            src_ref=picked.at[index, step],
-            dst_ref=halves.at[index, me],
-            send_sem=pick_send.at[index, step],
-            recv_sem=pick_recv.at[index, step],
-            device_id=(pole, core, peer),
+    def mate(step):
+        return base + lax.rem(me - base + 1 + step, mates + 1)
+
+    def mirror_copy(part):
+        piece = pl.ds(part * span, span)
+        return pltpu.make_async_remote_copy(
+            src_ref=lower_ref.at[piece],
+            dst_ref=mirrored.at[piece],
+            send_sem=mirror_send.at[part],
+            recv_sem=mirror_recv.at[part],
+            device_id=(pole, core, mirror),
+            device_id_type=MESH,
+        )
+
+    def pick_copy(relayed, index, step):
+        return pltpu.make_async_remote_copy(
+            src_ref=picked.at[relayed, index, step],
+            dst_ref=halves.at[index, mirror if relayed else me],
+            send_sem=pick_send.at[relayed, index, step],
+            recv_sem=pick_recv.at[relayed, index, step],
+            device_id=(pole, core, mate(step)),
             device_id_type=MESH,
         )
 
@@ -132,25 +153,37 @@
             device_id_type=MESH,
         )
 
-    def send_task(index, carry):
-        def to_peer(step, inner):
-            peer = lax.rem(me + 1 + step, columns)
-            picked[index, step] = lower_ref[tasks[peer * cap + index]]
-            pick_copy(index, step).start()
-            return inner
-
-        lax.fori_loop(0, peers, to_peer, 0)
-        halves[index, me] = lower_ref[tasks[me * cap + index]]
-        return carry
-
-    lax.fori_loop(0, cap, send_task, 0)
+    def send_tasks(relayed, source):
+        def send_task(index, carry):
+            def to_mate(step, inner):
+                picked[relayed, index, step] = source[tasks[mate(step) * cap + index]]
+                pick_copy(relayed, index, step).start()
+                return inner
+
+            lax.fori_loop(0, mates, to_mate, 0)
+            halves[index, mirror if relayed else me] = source[tasks[me * cap + index]]
+            return carry
+
+        lax.fori_loop(0, cap, send_task, 0)
+
+    for part in range(parts):
+        mirror_copy(part).start()
+    load_inverse.start()
+    load_diag.start()
+    send_tasks(0, lower_ref)
+    for part in range(parts):
+        mirror_copy(part).wait_recv()
+    send_tasks(1, mirrored)
+    load_inverse.wait()
+    load_diag.wait()
 
     def arrive(index):
         def one(step, inner):
-            pick_copy(index, step).wait_recv()
-            return inner
-
-        lax.fori_loop(0, peers, one, 0)
+            pick_copy(0, index, step).wait_recv()
+            pick_copy(1, index, step).wait_recv()
+            return inner
+
+        lax.fori_loop(0, mates, one, 0)
         chosen_slot = own_slot[me * cap + index]
         mine = halves[index, :, 0]
         for slot in range(1, slots):
@@ -225,17 +258,24 @@
     lax.fori_loop(0, nodes, finish, 0)
 
     def sent(index, carry):
-        def one(step, inner):
-            pick_copy(index, step).wait_send()
+        def one_pick(step, inner):
+            pick_copy(0, index, step).wait_send()
+            pick_copy(1, index, step).wait_send()
+            return inner
+
+        def one_out(step, inner):
             out_copy(index, step).wait_send()
             return inner
 
-        lax.fori_loop(0, peers, one, 0)
+        lax.fori_loop(0, mates, one_pick, 0)
+        lax.fori_loop(0, peers, one_out, 0)
         half_copy(index).wait_send()
         core_copy(index).wait_send()
         return carry
 
     lax.fori_loop(0, cap, sent, 0)
+    for part in range(parts):
+        mirror_copy(part).wait_send()
 
 
 def per_device_fused(inverse_blocks, lower, diag_inverse, structure):
@@ -259,23 +299,32 @@
     places = jnp.sum(jnp.where(matches, position[:, :, None], 0), axis=0)
     smem = pl.BlockSpec(memory_space=pltpu.SMEM)
     vmem = pl.BlockSpec(memory_space=pltpu.VMEM)
+    anywhere = pl.BlockSpec(memory_space=pl.ANY)
     peers = columns - 1
+    mates = columns // 2 - 1
+    parts = 4 if nodes % 4 == 0 else 1
     dma = pltpu.SemaphoreType.DMA
     return pl.pallas_call(
         functools.partial(fused_kernel, columns, cap, nodes, slots),
         out_shape=jax.ShapeDtypeStruct(diag_inverse.shape, jnp.float32),
-        in_specs=[smem] * 4 + [vmem] * 3,
+        in_specs=[smem] * 4 + [anywhere, vmem, anywhere],
         out_specs=vmem,
         scratch_shapes=[
-            pltpu.VMEM((cap, peers, slots, chunk, B), jnp.bfloat16),
+            pltpu.VMEM(inverse_blocks.shape, jnp.bfloat16),
+            pltpu.VMEM(diag_inverse.shape, jnp.float32),
+            pltpu.VMEM(lower.shape, jnp.bfloat16),
+            pltpu.VMEM((2, cap, mates, slots, chunk, B), jnp.bfloat16),
             pltpu.VMEM((cap, columns, slots, chunk, B), jnp.bfloat16),
             pltpu.VMEM((cap, 2, B // 2, B), jnp.bfloat16),
             pltpu.VMEM((cap, 2, B // 2, B), jnp.float32),
             pltpu.VMEM((cap, B // 2, B), jnp.float32),
             pltpu.VMEM((cap, columns, chunk, B), jnp.bfloat16),
             pltpu.VMEM((columns, cap, chunk, B), jnp.bfloat16),
-            dma((cap, peers)),
-            dma((cap, peers)),
+            dma((2,)),
+            dma((parts,)),
+            dma((parts,)),
+            dma((2, cap, mates)),
+            dma((2, cap, mates)),
             dma((cap,)),
             dma((cap,)),
             dma((cap,)),

time: 175 us -> 147 us (0.84)
  Pallas kernels: 167 us -> 138 us
    pallas_call x1, Pallas kernels: 167 us -> 138 us  [per_device_fused(): pl.pallas_call(functools.partial(fused_kernel, columns, cap, nodes, slots...]
where the time goes in v2:
time: 147 us
  Pallas kernels  138 us (94%)
  local copies, waits for them, and re-layouts  6.55 us (4%)
  other arithmetic  1.93 us (1%)
    pallas_call x1, Pallas kernels, per_device_fused(): pl.pallas_call(functools.partial(fused_kernel, columns, cap, nodes, slots...  138 us
    unnamed x8, local copies, waits for them, and re-layouts  5.95 us

profile of v2, /device:TPU:0, one launch (start us, length us, event | category | flops | bytes accessed | tf_op | source)
XLA Modules:
  0.0 146.6 jit_solution(16908510550650939809)
XLA Ops:
  0.0 0.7 fusion.1
  0.7 0.2 convert_reduce_fusion
  0.9 0.7 select_reduce_fusion.2
  1.6 0.3 select_reduce_fusion
  1.9 0.1 copy.10
  2.0 0.1 reshape.30.own_slot
  2.1 0.1 copy.9
  2.2 0.1 reshape.29.tasks
  2.3 0.1 copy.12
  2.3 0.1 reshape.32.places
  2.4 0.8 copy.11
  3.2 0.1 reshape.31.structure
  3.3 0.0 copy-start
  3.3 1.6 %copy-done = bf16[8,256,512]{2,1,0:T(8,128)(2,1)S(1)} copy-done((bf16[8,256,512]{2,1,0:T(8,128)(2,1)S(1)}, bf16[8,256,512]{2,1,0:T(8,128)(2,1)}, u32[]{:S(2)}) %copy-start) | copy-done | bytes 2097176
  4.9 0.0 copy-start.1
  4.9 1.4 copy-done.1
  6.3 0.0 copy-start.2
  6.3 1.2 copy-done.2
  7.5 138.1 %shard_map.46 = f32[16,32,512]{2,1,0:T(8,128)S(1)} custom-call(s32[56]{0:T(128)S(1)} %reshape.29.tasks, s32[56]{0:T(128)S(1)} %reshape.30.own_slot, s32[48]{0:T(128)S(1)} %reshape.31.structure, s32[48]{0:T(128)S(1)} %reshape.32.places, bf16[8,256,512]{2,1,0:T(8,128)(2,1)S(1)} %copy-done, bf16[16,3,32,512]{3,2,1,0:T(8,128)(2,1)S(1)} %copy-done.1, ...), custom_call_target="tpu_custom_call" | custom-call | tf_op jit(solution)/shard_map/pallas_call | solution.py:307
  145.6 1.0 copy.14
  (1 shorter events, 0.0 us)
Async XLA Ops:
  3.3 1.6 %copy-start = (bf16[8,256,512]{2,1,0:T(8,128)(2,1)S(1)}, bf16[8,256,512]{2,1,0:T(8,128)(2,1)}, u32[]{:S(2)}) copy-start(bf16[8,256,512]{2,1,0:T(8,128)(2,1)} %inverse_hbm.1) | copy-start | bytes 6291460
  4.9 1.4 copy-start.1
  6.3 1.2 copy-start.2

commit v3 on v2

--- a/solution.py
+++ b/solution.py
@@ -79,6 +79,7 @@
     other = 1 - core
     peers = columns - 1
     mates = columns // 2 - 1
+    ahead = min(2, cap)
     base = (me // (mates + 1)) * (mates + 1)
     mirror = columns - 2 - me + 2 * (me % 2)
     parts = mirror_send.shape[0]
@@ -153,27 +154,28 @@
             device_id_type=MESH,
         )
 
-    def send_tasks(relayed, source):
-        def send_task(index, carry):
-            def to_mate(step, inner):
-                picked[relayed, index, step] = source[tasks[mate(step) * cap + index]]
-                pick_copy(relayed, index, step).start()
-                return inner
-
-            lax.fori_loop(0, mates, to_mate, 0)
-            halves[index, mirror if relayed else me] = source[tasks[me * cap + index]]
-            return carry
-
-        lax.fori_loop(0, cap, send_task, 0)
+    def send_task(relayed, source, index):
+        def to_mate(step, inner):
+            picked[relayed, index, step] = source[tasks[mate(step) * cap + index]]
+            pick_copy(relayed, index, step).start()
+            return inner
+
+        lax.fori_loop(0, mates, to_mate, 0)
+        halves[index, mirror if relayed else me] = source[tasks[me * cap + index]]
+
+    def send_own(index, carry):
+        send_task(0, lower_ref, index)
+        return carry
 
     for part in range(parts):
         mirror_copy(part).start()
     load_inverse.start()
     load_diag.start()
-    send_tasks(0, lower_ref)
+    lax.fori_loop(0, cap, send_own, 0)
     for part in range(parts):
         mirror_copy(part).wait_recv()
-    send_tasks(1, mirrored)
+    for index in range(ahead):
+        send_task(1, mirrored, index)
     load_inverse.wait()
     load_diag.wait()
 
@@ -224,6 +226,10 @@
         @pl.when(step < cap)
         def _():
             arrive(step)
+
+        @pl.when(step < cap - ahead)
+        def _():
+            send_task(1, mirrored, step + ahead)
 
         @pl.when((step >= 1) & (step < cap + 1))
         def _():

time: 147 us -> 150 us (1.020)
  Pallas kernels: 138 us -> 140 us
    pallas_call x1, Pallas kernels: 138 us -> 140 us  [per_device_fused(): pl.pallas_call(functools.partial(fused_kernel, columns, cap, nodes, slots...]
where the time goes in v3:
time: 150 us; the launch traced here: 149 us
  Pallas kernels  140 us (93%)
  local copies, waits for them, and re-layouts  6.55 us (4%)
  other arithmetic  1.93 us (1%)
    pallas_call x1, Pallas kernels, per_device_fused(): pl.pallas_call(functools.partial(fused_kernel, columns, cap, nodes, slots...  140 us
    unnamed x8, local copies, waits for them, and re-layouts  5.95 us

profile of v3, /device:TPU:0, one launch (start us, length us, event | category | flops | bytes accessed | tf_op | source)
XLA Modules:
  0.0 148.5 jit_solution(18393823259982810486)
XLA Ops:
  0.0 0.7 fusion.1
  0.7 0.2 convert_reduce_fusion
  0.9 0.7 select_reduce_fusion.2
  1.6 0.3 select_reduce_fusion
  1.9 0.1 copy.10
  2.0 0.1 reshape.30.own_slot
  2.1 0.1 copy.9
  2.2 0.1 reshape.29.tasks
  2.3 0.1 copy.12
  2.3 0.1 reshape.32.places
  2.4 0.8 copy.11
  3.2 0.1 reshape.31.structure
  3.3 0.0 copy-start
  3.3 1.6 %copy-done = bf16[8,256,512]{2,1,0:T(8,128)(2,1)S(1)} copy-done((bf16[8,256,512]{2,1,0:T(8,128)(2,1)S(1)}, bf16[8,256,512]{2,1,0:T(8,128)(2,1)}, u32[]{:S(2)}) %copy-start) | copy-done | bytes 2097176
  4.9 0.0 copy-start.1
  4.9 1.4 copy-done.1
  6.3 0.0 copy-start.2
  6.3 1.2 copy-done.2
  7.5 140.0 %shard_map.46 = f32[16,32,512]{2,1,0:T(8,128)S(1)} custom-call(s32[56]{0:T(128)S(1)} %reshape.29.tasks, s32[56]{0:T(128)S(1)} %reshape.30.own_slot, s32[48]{0:T(128)S(1)} %reshape.31.structure, s32[48]{0:T(128)S(1)} %reshape.32.places, bf16[8,256,512]{2,1,0:T(8,128)(2,1)S(1)} %copy-done, bf16[16,3,32,512]{3,2,1,0:T(8,128)(2,1)S(1)} %copy-done.1, ...), custom_call_target="tpu_custom_call" | custom-call | tf_op jit(solution)/shard_map/pallas_call | solution.py:313
  147.6 1.0 copy.14
  (1 shorter events, 0.0 us)
Async XLA Ops:
  3.3 1.6 %copy-start = (bf16[8,256,512]{2,1,0:T(8,128)(2,1)S(1)}, bf16[8,256,512]{2,1,0:T(8,128)(2,1)}, u32[]{:S(2)}) copy-start(bf16[8,256,512]{2,1,0:T(8,128)(2,1)} %inverse_hbm.1) | copy-start | bytes 6291460
  4.9 1.4 copy-start.1
  6.3 1.2 copy-start.2

commit v4 on v2

--- a/solution.py
+++ b/solution.py
@@ -70,8 +70,10 @@
     tasks, own_slot, structure, places,
     inverse_hbm, lower_ref, diag_hbm,
     out_ref,
-    inverse_ref, diag_ref, mirrored, picked, halves, full, partial, from_core, outgoing, incoming,
-    load_sem, mirror_send, mirror_recv, pick_send, pick_recv, half_send, half_recv, core_send, core_recv, out_send, out_recv,
+    inverse_ref, diag_ref, picked, relayed, halves, full, partial, from_core, outgoing, incoming,
+    load_sem, mirror_send, mirror_recv, pick_send, pick_recv, relay_send, relay_recv,
+    half_send, half_recv, core_send, core_recv, out_send, out_recv,
+    *mirrored,
 ):
     pole = lax.axis_index("pole")
     core = lax.axis_index("prow")
@@ -81,8 +83,6 @@
     mates = columns // 2 - 1
     base = (me // (mates + 1)) * (mates + 1)
     mirror = columns - 2 - me + 2 * (me % 2)
-    parts = mirror_send.shape[0]
-    span = nodes // parts
 
     load_inverse = pltpu.make_async_copy(inverse_hbm, inverse_ref, load_sem.at[0])
     load_diag = pltpu.make_async_copy(diag_hbm, diag_ref, load_sem.at[1])
@@ -101,23 +101,32 @@
     def mate(step):
         return base + lax.rem(me - base + 1 + step, mates + 1)
 
-    def mirror_copy(part):
-        piece = pl.ds(part * span, span)
-        return pltpu.make_async_remote_copy(
-            src_ref=lower_ref.at[piece],
-            dst_ref=mirrored.at[piece],
-            send_sem=mirror_send.at[part],
-            recv_sem=mirror_recv.at[part],
+    def mirror_copy(slot):
+        return pltpu.make_async_remote_copy(
+            src_ref=lower_ref.at[:, slot],
+            dst_ref=mirrored[slot],
+            send_sem=mirror_send.at[slot],
+            recv_sem=mirror_recv.at[slot],
             device_id=(pole, core, mirror),
             device_id_type=MESH,
         )
 
-    def pick_copy(relayed, index, step):
-        return pltpu.make_async_remote_copy(
-            src_ref=picked.at[relayed, index, step],
-            dst_ref=halves.at[index, mirror if relayed else me],
-            send_sem=pick_send.at[relayed, index, step],
-            recv_sem=pick_recv.at[relayed, index, step],
+    def pick_copy(index, step):
+        return pltpu.make_async_remote_copy(
+            src_ref=picked.at[index, step],
+            dst_ref=halves.at[index, me],
+            send_sem=pick_send.at[index, step],
+            recv_sem=pick_recv.at[index, step],
+            device_id=(pole, core, mate(step)),
+            device_id_type=MESH,
+        )
+
+    def relay_copy(slot, index, step):
+        return pltpu.make_async_remote_copy(
+            src_ref=relayed.at[slot, index, step],
+            dst_ref=halves.at[index, mirror, slot],
+            send_sem=relay_send.at[slot, index, step],
+            recv_sem=relay_recv.at[slot, index, step],
             device_id=(pole, core, mate(step)),
             device_id_type=MESH,
         )
@@ -153,34 +162,45 @@
             device_id_type=MESH,
         )
 
-    def send_tasks(relayed, source):
-        def send_task(index, carry):
+    def send_own(index, carry):
+        def to_mate(step, inner):
+            picked[index, step] = lower_ref[tasks[mate(step) * cap + index]]
+            pick_copy(index, step).start()
+            return inner
+
+        lax.fori_loop(0, mates, to_mate, 0)
+        halves[index, me] = lower_ref[tasks[me * cap + index]]
+        return carry
+
+    def relay_slot(slot):
+        def relay_task(index, carry):
             def to_mate(step, inner):
-                picked[relayed, index, step] = source[tasks[mate(step) * cap + index]]
-                pick_copy(relayed, index, step).start()
+                relayed[slot, index, step] = mirrored[slot][tasks[mate(step) * cap + index]]
+                relay_copy(slot, index, step).start()
                 return inner
 
             lax.fori_loop(0, mates, to_mate, 0)
-            halves[index, mirror if relayed else me] = source[tasks[me * cap + index]]
+            halves[index, mirror, slot] = mirrored[slot][tasks[me * cap + index]]
             return carry
 
-        lax.fori_loop(0, cap, send_task, 0)
-
-    for part in range(parts):
-        mirror_copy(part).start()
+        lax.fori_loop(0, cap, relay_task, 0)
+
+    for slot in range(slots):
+        mirror_copy(slot).start()
     load_inverse.start()
     load_diag.start()
-    send_tasks(0, lower_ref)
-    for part in range(parts):
-        mirror_copy(part).wait_recv()
-    send_tasks(1, mirrored)
+    lax.fori_loop(0, cap, send_own, 0)
+    for slot in range(slots):
+        mirror_copy(slot).wait_recv()
+        relay_slot(slot)
     load_inverse.wait()
     load_diag.wait()
 
     def arrive(index):
         def one(step, inner):
-            pick_copy(0, index, step).wait_recv()
-            pick_copy(1, index, step).wait_recv()
+            pick_copy(index, step).wait_recv()
+            for slot in range(slots):
+                relay_copy(slot, index, step).wait_recv()
             return inner
 
         lax.fori_loop(0, mates, one, 0)
@@ -259,8 +279,9 @@
 
     def sent(index, carry):
         def one_pick(step, inner):
-            pick_copy(0, index, step).wait_send()
-            pick_copy(1, index, step).wait_send()
+            pick_copy(index, step).wait_send()
+            for slot in range(slots):
+                relay_copy(slot, index, step).wait_send()
             return inner
 
         def one_out(step, inner):
@@ -274,8 +295,8 @@
         return carry
 
     lax.fori_loop(0, cap, sent, 0)
-    for part in range(parts):
-        mirror_copy(part).wait_send()
+    for slot in range(slots):
+        mirror_copy(slot).wait_send()
 
 
 def per_device_fused(inverse_blocks, lower, diag_inverse, structure):
@@ -302,7 +323,6 @@
     anywhere = pl.BlockSpec(memory_space=pl.ANY)
     peers = columns - 1
     mates = columns // 2 - 1
-    parts = 4 if nodes % 4 == 0 else 1
     dma = pltpu.SemaphoreType.DMA
     return pl.pallas_call(
         functools.partial(fused_kernel, columns, cap, nodes, slots),
@@ -312,8 +332,8 @@
         scratch_shapes=[
             pltpu.VMEM(inverse_blocks.shape, jnp.bfloat16),
             pltpu.VMEM(diag_inverse.shape, jnp.float32),
-            pltpu.VMEM(lower.shape, jnp.bfloat16),
-            pltpu.VMEM((2, cap, mates, slots, chunk, B), jnp.bfloat16),
+            pltpu.VMEM((cap, mates, slots, chunk, B), jnp.bfloat16),
+            pltpu.VMEM((slots, cap, mates, chunk, B), jnp.bfloat16),
             pltpu.VMEM((cap, columns, slots, chunk, B), jnp.bfloat16),
             pltpu.VMEM((cap, 2, B // 2, B), jnp.bfloat16),
             pltpu.VMEM((cap, 2, B // 2, B), jnp.float32),
@@ -321,17 +341,20 @@
             pltpu.VMEM((cap, columns, chunk, B), jnp.bfloat16),
             pltpu.VMEM((columns, cap, chunk, B), jnp.bfloat16),
             dma((2,)),
-            dma((parts,)),
-            dma((parts,)),
-            dma((2, cap, mates)),
-            dma((2, cap, mates)),
+            dma((slots,)),
+            dma((slots,)),
+            dma((cap, mates)),
+            dma((cap, mates)),
+            dma((slots, cap, mates)),
+            dma((slots, cap, mates)),
             dma((cap,)),
             dma((cap,)),
             dma((cap,)),
             dma((cap,)),
             dma((cap, peers)),
             dma((cap, peers)),
-        ],
+        ]
+        + [pltpu.VMEM((nodes, chunk, B), jnp.bfloat16)] * slots,
         compiler_params=pltpu.CompilerParams(
             collective_id=0, has_side_effects=True, vmem_limit_bytes=48 * 1024 * 1024
         ),

time: 147 us -> 150 us (1.020)
  Pallas kernels: 138 us -> 142 us
    pallas_call x1, Pallas kernels: 138 us -> 142 us  [per_device_fused(): pl.pallas_call(functools.partial(fused_kernel, columns, cap, nodes, slots...]
where the time goes in v4:
time: 150 us
  Pallas kernels  142 us (95%)
  local copies, waits for them, and re-layouts  6.55 us (4%)
  other arithmetic  1.93 us (1%)
    pallas_call x1, Pallas kernels, per_device_fused(): pl.pallas_call(functools.partial(fused_kernel, columns, cap, nodes, slots...  142 us
    unnamed x8, local copies, waits for them, and re-layouts  5.95 us

profile of v4, /device:TPU:0, one launch (start us, length us, event | category | flops | bytes accessed | tf_op | source)
XLA Modules:
  0.0 150.0 jit_solution(10232506844377094867)
XLA Ops:
  0.0 0.7 fusion.1
  0.7 0.2 convert_reduce_fusion
  0.9 0.7 select_reduce_fusion.2
  1.6 0.3 select_reduce_fusion
  1.9 0.1 copy.10
  2.0 0.1 reshape.30.own_slot
  2.1 0.1 copy.9
  2.2 0.1 reshape.29.tasks
  2.3 0.1 copy.12
  2.3 0.1 reshape.32.places
  2.4 0.8 copy.11
  3.2 0.1 reshape.31.structure
  3.3 0.0 copy-start
  3.3 1.6 %copy-done = bf16[8,256,512]{2,1,0:T(8,128)(2,1)S(1)} copy-done((bf16[8,256,512]{2,1,0:T(8,128)(2,1)S(1)}, bf16[8,256,512]{2,1,0:T(8,128)(2,1)}, u32[]{:S(2)}) %copy-start) | copy-done | bytes 2097176
  4.9 0.0 copy-start.1
  4.9 1.4 copy-done.1
  6.3 0.0 copy-start.2
  6.3 1.2 copy-done.2
  7.5 141.5 %shard_map.46 = f32[16,32,512]{2,1,0:T(8,128)S(1)} custom-call(s32[56]{0:T(128)S(1)} %reshape.29.tasks, s32[56]{0:T(128)S(1)} %reshape.30.own_slot, s32[48]{0:T(128)S(1)} %reshape.31.structure, s32[48]{0:T(128)S(1)} %reshape.32.places, bf16[8,256,512]{2,1,0:T(8,128)(2,1)S(1)} %copy-done, bf16[16,3,32,512]{3,2,1,0:T(8,128)(2,1)S(1)} %copy-done.1, ...), custom_call_target="tpu_custom_call" | custom-call | tf_op jit(solution)/shard_map/pallas_call | solution.py:327
  149.1 1.0 copy.14
  (1 shorter events, 0.0 us)
Async XLA Ops:
  3.3 1.6 %copy-start = (bf16[8,256,512]{2,1,0:T(8,128)(2,1)S(1)}, bf16[8,256,512]{2,1,0:T(8,128)(2,1)}, u32[]{:S(2)}) copy-start(bf16[8,256,512]{2,1,0:T(8,128)(2,1)} %inverse_hbm.1) | copy-start | bytes 6291460
  4.9 1.4 copy-start.1
  6.3 1.2 copy-start.2

commit v5 on v2

--- a/solution.py
+++ b/solution.py
@@ -195,16 +195,18 @@
         half_copy(index).wait_recv()
         node = tasks[me * cap + index]
         factor = full[index].reshape(B, B)
-        total = jnp.zeros((B, B), jnp.float32)
-        for slot in range(slots):
-            chosen = inverse_ref[structure[node * slots + slot]]
-            products = jnp.dot(chosen, factor, preferred_element_type=jnp.float32).astype(
-                jnp.bfloat16
-            )
-            rows = halves[index, :, slot].reshape(B // 2, B)
-            total = total + lax.dot_general(
-                rows, products, (((0,), (0,)), ((), ())), preferred_element_type=jnp.float32
-            )
+        chosen = jnp.concatenate(
+            [inverse_ref[structure[node * slots + slot]] for slot in range(slots)], axis=0
+        )
+        products = jnp.dot(chosen, factor, preferred_element_type=jnp.float32).astype(
+            jnp.bfloat16
+        )
+        rows = jnp.concatenate(
+            [halves[index, :, slot].reshape(B // 2, B) for slot in range(slots)], axis=0
+        )
+        total = lax.dot_general(
+            rows, products, (((0,), (0,)), ((), ())), preferred_element_type=jnp.float32
+        )
         partial[index] = total.reshape(partial.shape[1:])
         core_copy(index).start()
 

time: 147 us -> 147 us (level)
  no operation moved by 1% of the time
where the time goes in v5:
time: 147 us
  Pallas kernels  138 us (94%)
  local copies, waits for them, and re-layouts  6.55 us (4%)
  other arithmetic  1.93 us (1%)
    pallas_call x1, Pallas kernels, per_device_fused(): pl.pallas_call(functools.partial(fused_kernel, columns, cap, nodes, slots...  138 us
    unnamed x8, local copies, waits for them, and re-layouts  5.95 us

profile of v5, /device:TPU:0, one launch (start us, length us, event | category | flops | bytes accessed | tf_op | source)
XLA Modules:
  0.0 146.6 jit_solution(6924515371096681787)
XLA Ops:
  0.0 0.7 fusion.1
  0.7 0.2 convert_reduce_fusion
  0.9 0.7 select_reduce_fusion.2
  1.6 0.3 select_reduce_fusion
  1.9 0.1 copy.10
  2.0 0.1 reshape.30.own_slot
  2.1 0.1 copy.9
  2.2 0.1 reshape.29.tasks
  2.3 0.1 copy.12
  2.3 0.1 reshape.32.places
  2.4 0.8 copy.11
  3.2 0.1 reshape.31.structure
  3.3 0.0 copy-start
  3.3 1.6 %copy-done = bf16[8,256,512]{2,1,0:T(8,128)(2,1)S(1)} copy-done((bf16[8,256,512]{2,1,0:T(8,128)(2,1)S(1)}, bf16[8,256,512]{2,1,0:T(8,128)(2,1)}, u32[]{:S(2)}) %copy-start) | copy-done | bytes 2097176
  4.9 0.0 copy-start.1
  4.9 1.4 copy-done.1
  6.3 0.0 copy-start.2
  6.3 1.2 copy-done.2
  7.5 138.0 %shard_map.46 = f32[16,32,512]{2,1,0:T(8,128)S(1)} custom-call(s32[56]{0:T(128)S(1)} %reshape.29.tasks, s32[56]{0:T(128)S(1)} %reshape.30.own_slot, s32[48]{0:T(128)S(1)} %reshape.31.structure, s32[48]{0:T(128)S(1)} %reshape.32.places, bf16[8,256,512]{2,1,0:T(8,128)(2,1)S(1)} %copy-done, bf16[16,3,32,512]{3,2,1,0:T(8,128)(2,1)S(1)} %copy-done.1, ...), custom_call_target="tpu_custom_call" | custom-call | tf_op jit(solution)/shard_map/pallas_call | solution.py:309
  145.6 1.0 copy.14
  (1 shorter events, 0.0 us)
Async XLA Ops:
  3.3 1.6 %copy-start = (bf16[8,256,512]{2,1,0:T(8,128)(2,1)S(1)}, bf16[8,256,512]{2,1,0:T(8,128)(2,1)}, u32[]{:S(2)}) copy-start(bf16[8,256,512]{2,1,0:T(8,128)(2,1)} %inverse_hbm.1) | copy-start | bytes 6291460
  4.9 1.4 copy-start.1
  6.3 1.2 copy-start.2

commit v6 on v3

--- a/solution.py
+++ b/solution.py
@@ -79,7 +79,7 @@
     other = 1 - core
     peers = columns - 1
     mates = columns // 2 - 1
-    ahead = min(2, cap)
+    ahead = min(4, cap)
     base = (me // (mates + 1)) * (mates + 1)
     mirror = columns - 2 - me + 2 * (me % 2)
     parts = mirror_send.shape[0]
@@ -197,16 +197,18 @@
         half_copy(index).wait_recv()
         node = tasks[me * cap + index]
         factor = full[index].reshape(B, B)
-        total = jnp.zeros((B, B), jnp.float32)
-        for slot in range(slots):
-            chosen = inverse_ref[structure[node * slots + slot]]
-            products = jnp.dot(chosen, factor, preferred_element_type=jnp.float32).astype(
-                jnp.bfloat16
-            )
-            rows = halves[index, :, slot].reshape(B // 2, B)
-            total = total + lax.dot_general(
-                rows, products, (((0,), (0,)), ((), ())), preferred_element_type=jnp.float32
-            )
+        chosen = jnp.concatenate(
+            [inverse_ref[structure[node * slots + slot]] for slot in range(slots)], axis=0
+        )
+        products = jnp.dot(chosen, factor, preferred_element_type=jnp.float32).astype(
+            jnp.bfloat16
+        )
+        rows = jnp.concatenate(
+            [halves[index, :, slot].reshape(B // 2, B) for slot in range(slots)], axis=0
+        )
+        total = lax.dot_general(
+            rows, products, (((0,), (0,)), ((), ())), preferred_element_type=jnp.float32
+        )
         partial[index] = total.reshape(partial.shape[1:])
         core_copy(index).start()
 

time: 150 us -> 147 us (0.980)
  Pallas kernels: 140 us -> 138 us
    pallas_call x1, Pallas kernels: 140 us -> 138 us  [per_device_fused(): pl.pallas_call(functools.partial(fused_kernel, columns, cap, nodes, slots...]
where the time goes in v6:
time: 147 us
  Pallas kernels  138 us (94%)
  local copies, waits for them, and re-layouts  6.55 us (4%)
  other arithmetic  1.93 us (1%)
    pallas_call x1, Pallas kernels, per_device_fused(): pl.pallas_call(functools.partial(fused_kernel, columns, cap, nodes, slots...  138 us
    unnamed x8, local copies, waits for them, and re-layouts  5.95 us

profile of v6, /device:TPU:0, one launch (start us, length us, event | category | flops | bytes accessed | tf_op | source)
XLA Modules:
  0.0 146.6 jit_solution(2346678162399671654)
XLA Ops:
  0.0 0.7 fusion.1
  0.7 0.2 convert_reduce_fusion
  0.9 0.7 select_reduce_fusion.2
  1.6 0.3 select_reduce_fusion
  1.9 0.1 copy.10
  2.0 0.1 reshape.30.own_slot
  2.1 0.1 copy.9
  2.2 0.1 reshape.29.tasks
  2.3 0.1 copy.12
  2.3 0.1 reshape.32.places
  2.4 0.8 copy.11
  3.2 0.1 reshape.31.structure
  3.3 0.0 copy-start
  3.3 1.6 %copy-done = bf16[8,256,512]{2,1,0:T(8,128)(2,1)S(1)} copy-done((bf16[8,256,512]{2,1,0:T(8,128)(2,1)S(1)}, bf16[8,256,512]{2,1,0:T(8,128)(2,1)}, u32[]{:S(2)}) %copy-start) | copy-done | bytes 2097176
  4.9 0.0 copy-start.1
  4.9 1.4 copy-done.1
  6.3 0.0 copy-start.2
  6.3 1.2 copy-done.2
  7.5 138.0 %shard_map.46 = f32[16,32,512]{2,1,0:T(8,128)S(1)} custom-call(s32[56]{0:T(128)S(1)} %reshape.29.tasks, s32[56]{0:T(128)S(1)} %reshape.30.own_slot, s32[48]{0:T(128)S(1)} %reshape.31.structure, s32[48]{0:T(128)S(1)} %reshape.32.places, bf16[8,256,512]{2,1,0:T(8,128)(2,1)S(1)} %copy-done, bf16[16,3,32,512]{3,2,1,0:T(8,128)(2,1)S(1)} %copy-done.1, ...), custom_call_target="tpu_custom_call" | custom-call | tf_op jit(solution)/shard_map/pallas_call | solution.py:315
  145.6 1.0 copy.14
  (1 shorter events, 0.0 us)
Async XLA Ops:
  3.3 1.6 %copy-start = (bf16[8,256,512]{2,1,0:T(8,128)(2,1)S(1)}, bf16[8,256,512]{2,1,0:T(8,128)(2,1)}, u32[]{:S(2)}) copy-start(bf16[8,256,512]{2,1,0:T(8,128)(2,1)} %inverse_hbm.1) | copy-start | bytes 6291460
  4.9 1.4 copy-start.1
  6.3 1.2 copy-start.2

commit v7 on v2

--- a/solution.py
+++ b/solution.py
@@ -143,7 +143,7 @@
         )
 
     def out_copy(index, step):
-        peer = lax.rem(me + 1 + step, columns)
+        peer = lax.rem(me + 1 + lax.rem(step + columns // 2 - 1, peers), columns)
         return pltpu.make_async_remote_copy(
             src_ref=outgoing.at[index, peer],
             dst_ref=incoming.at[me, index],

time: 147 us -> 147 us (level)
  no operation moved by 1% of the time
where the time goes in v7:
time: 147 us
  Pallas kernels  139 us (95%)
  local copies, waits for them, and re-layouts  6.55 us (4%)
  other arithmetic  1.93 us (1%)
    pallas_call x1, Pallas kernels, per_device_fused(): pl.pallas_call(functools.partial(fused_kernel, columns, cap, nodes, slots...  139 us
    unnamed x8, local copies, waits for them, and re-layouts  5.95 us

profile of v7, /device:TPU:0, one launch (start us, length us, event | category | flops | bytes accessed | tf_op | source)
XLA Modules:
  0.0 147.2 jit_solution(11416141184060489924)
XLA Ops:
  0.0 0.7 fusion.1
  0.7 0.2 convert_reduce_fusion
  0.9 0.7 select_reduce_fusion.2
  1.6 0.3 select_reduce_fusion
  1.9 0.1 copy.10
  2.0 0.1 reshape.30.own_slot
  2.1 0.1 copy.9
  2.2 0.1 reshape.29.tasks
  2.3 0.1 copy.12
  2.3 0.1 reshape.32.places
  2.4 0.8 copy.11
  3.2 0.1 reshape.31.structure
  3.3 0.0 copy-start
  3.3 1.6 %copy-done = bf16[8,256,512]{2,1,0:T(8,128)(2,1)S(1)} copy-done((bf16[8,256,512]{2,1,0:T(8,128)(2,1)S(1)}, bf16[8,256,512]{2,1,0:T(8,128)(2,1)}, u32[]{:S(2)}) %copy-start) | copy-done | bytes 2097176
  4.9 0.0 copy-start.1
  4.9 1.4 copy-done.1
  6.3 0.0 copy-start.2
  6.3 1.2 copy-done.2
  7.5 138.7 %shard_map.46 = f32[16,32,512]{2,1,0:T(8,128)S(1)} custom-call(s32[56]{0:T(128)S(1)} %reshape.29.tasks, s32[56]{0:T(128)S(1)} %reshape.30.own_slot, s32[48]{0:T(128)S(1)} %reshape.31.structure, s32[48]{0:T(128)S(1)} %reshape.32.places, bf16[8,256,512]{2,1,0:T(8,128)(2,1)S(1)} %copy-done, bf16[16,3,32,512]{3,2,1,0:T(8,128)(2,1)S(1)} %copy-done.1, ...), custom_call_target="tpu_custom_call" | custom-call | tf_op jit(solution)/shard_map/pallas_call | solution.py:307
  146.2 1.0 copy.14
  (1 shorter events, 0.0 us)
Async XLA Ops:
  3.3 1.6 %copy-start = (bf16[8,256,512]{2,1,0:T(8,128)(2,1)S(1)}, bf16[8,256,512]{2,1,0:T(8,128)(2,1)}, u32[]{:S(2)}) copy-start(bf16[8,256,512]{2,1,0:T(8,128)(2,1)} %inverse_hbm.1) | copy-start | bytes 6291460
  4.9 1.4 copy-start.1
  6.3 1.2 copy-start.2
